TPU v7x, 512 devices: a whole 4x8x8 slice. The times are simulated.
512 devices in a mesh: member: 16 (over y, core), grid: 32 (over x, z).
Axes of the slice: x: 4, y: 8, z: 8, core: 2. Of those that a mesh axis runs over, the one named last changes fastest.
Arguments:
- latents: bfloat16 [16, 1536, 1024], P('member', 'grid'), may hold values from -6 to 6
- dst_embed: bfloat16 [8192, 1024], P('grid'), may hold values from -6 to 6
- w_msg: bfloat16 [1024, 1024], replicated, may hold values from -0.1875 to 0.1875
- w_out: bfloat16 [1024, 128], replicated, may hold values from -0.1875 to 0.1875
- need_rows: int32 [96, 32], P('grid'), may hold values from 0 to 47, as said below
- edge_src: int32 [24576], P('grid'), may hold values from 0 to 95, as said below
- edge_dst: int32 [24576], P('grid'), may hold values from 0 to 255
- edge_count: int32 [32], P('grid'), may hold values from 96 to 768, as said below
- target: float32 [8192, 128], P('grid'), may hold values from -6 to 6
- point_weight: float32 [8192], P('grid')
- field_weight: float32 [128], replicated, may hold values from 0.3 to 3
Outputs:
- grad_latents: float32 [16, 1536, 1024], P('member', 'grid')
Inputs may be any that keep to these rules, and one draw needn't show every extreme that they name: `need_rows`: row 3 g + r lists 32 distinct mesh nodes, as indices within shard (g + r - 1) mod 32, that grid shard g reads. `edge_src`: slot q of an edge reads request row q // 32 of its shard: 0 the shard before it, 1 its own, 2 the shard after it (cyclically). Grid shard g's first edge_count[g] edges are live and the rest are padding; some grid shard has all 768 live.
All inputs are finite; a program needn't handle non-finite values.
Results may differ from a plain program's by a relative error of at most 0.0095.
Values may be sent and summed in bfloat16 or wider, within the bound.
A program may use at most 64 MiB of HBM per device.

v0:
```python
import jax
import jax.numpy as jnp
from jax import lax
from jax.sharding import PartitionSpec as P

smooth_width = 0.1
norm_eps = 1e-06


def padded(array, sides, width):
    for axis, dim in sides:
        size, length = (lax.axis_size(axis), array.shape[dim])
        up = [(i, (i + 1) % size) for i in range(size)]
        down = [(j, i) for i, j in up]
        last = lax.slice_in_dim(array, length - width, length, axis=dim)
        initial = lax.slice_in_dim(array, 0, width, axis=dim)
        before = lax.ppermute(last, axis, up)
        after = lax.ppermute(initial, axis, down)
        array = jnp.concatenate([before, array, after], axis=dim)
    return array


def smooth_abs(gaps):
    return jnp.sqrt(gaps * gaps + smooth_width * smooth_width)


def smooth_slope(gaps):
    return gaps / smooth_abs(gaps)


def pre_inputs(slot_rows, dst_embed, source_slots, dest_rows):
    return jnp.take(slot_rows, source_slots, axis=0).astype(jnp.float32) + jnp.take(
        dst_embed, dest_rows, axis=0
    ).astype(jnp.float32)


def edge_messages(pre_act, w_msg):
    hidden = jax.nn.silu(pre_act).astype(jnp.bfloat16)
    return jnp.dot(hidden, w_msg, preferred_element_type=jnp.float32).astype(jnp.bfloat16)


def spread_points(message, dest_rows, live_mask, points):
    onehot = (dest_rows[None, :] == jnp.arange(points, dtype=jnp.int32)[:, None]) & live_mask[
        None, :
    ]
    return jnp.dot(onehot.astype(jnp.bfloat16), message, preferred_element_type=jnp.float32)


def edge_grads(pre_act, grad_summed, dest_rows, live_mask, w_msg):
    grad_message = jnp.where(
        live_mask[:, None], jnp.take(grad_summed, dest_rows, axis=0), jnp.zeros((), jnp.bfloat16)
    )
    grad_hidden = lax.dot_general(
        grad_message, w_msg, (((1,), (1,)), ((), ())), preferred_element_type=jnp.float32
    )
    sigma = jax.nn.sigmoid(pre_act)
    return (grad_hidden * sigma * (1.0 + pre_act * (1.0 - sigma))).astype(jnp.bfloat16)


def local(
    latents,
    dst_embed,
    w_msg,
    w_out,
    need_rows,
    edge_src,
    edge_dst,
    edge_count,
    target,
    point_weight,
    field_weight,
):
    slots = need_rows.shape[1]
    node_dev = latents.shape[1]
    points = dst_embed.shape[0]
    width = dst_embed.shape[1]
    edges = edge_src.shape[0]
    slot_total = 3 * slots
    latent_rows = latents[0]
    table = padded(latent_rows, (("grid", 0),), node_dev)
    node_ids = (jnp.arange(3, dtype=jnp.int32)[:, None] * node_dev + need_rows).reshape(-1)
    slot_rows = jnp.take(table, node_ids, axis=0)
    live_count = edge_count[0]
    live_mask = jnp.arange(edges, dtype=jnp.int32) < live_count
    pre_act = pre_inputs(slot_rows, dst_embed, edge_src, edge_dst)
    summed = spread_points(edge_messages(pre_act, w_msg), edge_dst, live_mask, points)
    inv_rms = lax.rsqrt(jnp.mean(summed * summed, axis=1, keepdims=True) + norm_eps)
    unit_rows = summed * inv_rms
    normed = unit_rows.astype(jnp.bfloat16)
    fields = jnp.dot(normed, w_out, preferred_element_type=jnp.float32)
    weights = point_weight[:, None] * field_weight[None, :]
    members = lax.axis_size("member")
    share = points // members
    first_point = lax.axis_index("member") * share
    ensemble = lax.all_to_all(fields[None], "member", split_axis=1, concat_axis=0, tiled=True)
    truth = lax.dynamic_slice_in_dim(target, first_point, share, 0)
    local_weights = lax.dynamic_slice_in_dim(weights, first_point, share, 0)
    gaps = ensemble[:, None] - ensemble[None]
    pair_slope = jnp.sum(smooth_slope(gaps), axis=1)
    member_grads = local_weights[None] * (
        smooth_slope(ensemble - truth[None]) - pair_slope / (members - 1)
    )
    grad_fields = lax.all_to_all(
        member_grads.astype(jnp.bfloat16), "member", split_axis=0, concat_axis=1, tiled=True
    ).astype(member_grads.dtype)[0]
    grad_cast = grad_fields.astype(jnp.bfloat16)
    grad_normed = lax.dot_general(
        grad_cast, w_out, (((1,), (1,)), ((), ())), preferred_element_type=jnp.float32
    )
    grad_summed = (
        inv_rms
        * (grad_normed - unit_rows * jnp.mean(grad_normed * unit_rows, axis=1, keepdims=True))
    ).astype(jnp.bfloat16)
    grad_pre = edge_grads(pre_act, grad_summed, edge_dst, live_mask, w_msg)
    slot_sums = jax.ops.segment_sum(grad_pre.astype(jnp.float32), edge_src, num_segments=slot_total)
    slot_grads = slot_sums.astype(jnp.bfloat16)
    placing = (jnp.arange(3 * node_dev, dtype=jnp.int32)[:, None] == node_ids[None, :]).astype(
        jnp.bfloat16
    )
    spread_rows = jnp.dot(placing, slot_grads, preferred_element_type=jnp.float32).reshape(
        3, node_dev, width
    )
    sending = jnp.stack([spread_rows[0], spread_rows[2]]).astype(jnp.bfloat16)
    returned = padded(sending, (("grid", 0),), 1)
    grad_latents = (
        returned[0].astype(jnp.float32) + spread_rows[1] + returned[-1].astype(jnp.float32)
    )
    return grad_latents[None]


def solution(mesh):
    placed = (
        P("member", "grid", None),
        P("grid", None),
        P(),
        P(),
        P("grid", None),
        P("grid"),
        P("grid"),
        P("grid"),
        P("grid", None),
        P("grid"),
        P(),
    )
    return jax.shard_map(
        local, mesh=mesh, in_specs=placed, out_specs=P("member", "grid", None), check_vma=False
    )
```

profile of v0, /device:TPU:1, one launch (start us, length us, event | category | flops | bytes accessed | tf_op | source)
XLA Modules:
  0.0 97.7 jit_solution(16481396516720625324)
XLA Ops:
  0.0 0.0 copy-start
  0.0 13.8 %collective-permute-start.1 = (bf16[48,1024]{1,0:T(8,128)(2,1)}, bf16[48,1024]{1,0:T(8,128)(2,1)S(1)}, u32[]{:S(2)}, u32[]{:S(2)}) collective-permute-start(bf16[48,1024]{1,0:T(8,128)(2,1)} %bitcast.28), channel_id=1, source_target_pairs={{1,0},{2,1},{3,2},{4,3},{5,4},{6,5},{7,6},{8,7},{9,8},{10,9},{11,1... | collective-permute-start | bytes 294920 | tf_op jit(solution)/shard_map/ppermute | solution.py:18
  13.8 1.9 %collective-permute-start = (bf16[48,1024]{1,0:T(8,128)(2,1)}, bf16[48,1024]{1,0:T(8,128)(2,1)S(1)}, u32[]{:S(2)}, u32[]{:S(2)}) collective-permute-start(bf16[48,1024]{1,0:T(8,128)(2,1)} %bitcast.29), channel_id=1, source_target_pairs={{0,1},{1,2},{2,3},{3,4},{4,5},{5,6},{6,7},{7,8},{8,9},{9,10},{10,1... | collective-permute-start | bytes 294920 | tf_op jit(solution)/shard_map/ppermute | solution.py:17
  15.8 0.8 broadcast_add_fusion
  16.5 0.1 eq.29
  16.6 0.0 copy-start.5
  16.6 0.1 reshape.100
  16.7 0.7 compare_and_fusion.1
  17.4 0.0 copy-start.7
  17.4 0.7 compare_select_fusion.1
  18.7 0.0 copy-done.5
  18.8 0.7 compare_select_fusion
  19.5 0.7 iota_compare_fusion.3
  20.2 0.0 copy-start.9
  20.2 0.0 copy-start.11
  20.2 0.0 copy-start.3
  20.2 5.7 %gather_fusion.2 = bf16[768,1024]{1,0:T(8,128)(2,1)} fusion(bf16[256,1024]{1,0:T(8,128)(2,1)} %param.14, s32[1024]{0:T(1024)S(1)} %pad_clamp_fusion), kind=kCustom, calls=%fused_computation.clone | custom fusion | bytes 3148800 | tf_op jit(solution)/shard_map/jit(_take)/gather | solution.py:32
  25.9 0.0 collective-permute-done.1
  25.9 0.0 collective-permute-done
  25.9 0.0 copy-done.3
  26.0 0.8 gather_fusion
  26.7 0.1 broadcast_select_fusion.6
  26.8 0.0 copy-start.4
  26.8 3.6 %gather_fusion.1 = bf16[768,1024]{1,0:T(8,128)(2,1)} fusion(bf16[96,1024]{1,0:T(8,128)(2,1)S(1)} %broadcast_select_fusion.6, s32[1024]{0:T(1024)S(1)} %pad_clamp_fusion.1), kind=kCustom, calls=%fused_computation.3 | custom fusion | bytes 3148800 | tf_op jit(solution)/shard_map/jit(_take)/gather | solution.py:32
  30.4 0.0 copy-done.7
  30.4 0.0 copy-done.9
  30.4 0.0 copy-done.11
  30.5 0.0 copy-done
  30.5 0.0 copy-done.4
  30.5 0.0 copy-start.2
  30.5 0.0 copy-start.13
  30.5 4.7 %multiply_reduce_fusion.1 = (f32[256]{0:T(256)S(1)}, f32[256,1024]{1,0:T(8,128)S(1)}) fusion(bf16[1024,1024]{1,0:T(8,128)(2,1)S(1)} %copy-done, bf16[768,1024]{1,0:T(8,128)(2,1)} %gather_fusion.2, pred[768]{0:T(1024)(128)(4,1)S(1)} %get-tuple-element.15, bf16[768,1024]{1,0:T(8,128)(2,1)} %gather_fusion.1, pred[768]{0:T(1024)(128)(4,1)S(1)} %compare_and_fusion.1, ...), kind=kOutput, calls=%fused_computation.25 | convolution fusion | flops 2022833920 | bytes 6297856 | tf_op jit(solution)/shard_map/dot_general | solution.py:46
  35.2 0.0 copy-start.1
  35.2 0.0 copy-done.2
  35.2 1.0 %fusion.12 = f32[256,128]{1,0:T(8,128)} fusion(bf16[1024,128]{1,0:T(8,128)(2,1)S(1)} %copy-done.2, f32[256,1024]{1,0:T(8,128)S(1)} %get-tuple-element.9, f32[256]{0:T(256)S(1)} %add_rsqrt_fusion), kind=kOutput, calls=%fused_computation.31 | convolution fusion | flops 67633152 | bytes 1442816 | tf_op jit(solution)/shard_map/dot_general | solution.py:90
  36.2 8.1 %all-to-all-start = ((f32[1,256,128]{2,0,1:T(1,128)}), f32[1,256,128]{2,0,1:T(1,128)S(1)}, u32[]{:S(2)}, u32[]{:S(2)}) async-start(f32[1,256,128]{2,0,1:T(1,128)} %bitcast.4), calls=%async_computation | async-start | bytes 262144 | tf_op jit(solution)/shard_map/all_to_all | solution.py:95
  44.3 0.0 copy-done.13
  44.3 0.1 dynamic-slice
  44.3 1.3 %broadcast_multiply_fusion = (f32[16,128]{1,0:T(8,128)S(1)}, f32[16,128]{1,0:T(8,128)}) fusion(f32[128]{0:T(128)} %param.23, f32[16]{0:T(128)S(1)} %dynamic-slice, f32[256,128]{1,0:T(8,128)} %param.21, s32[]{:T(128)S(6)} %select_n.48), kind=kLoop, calls=%fused_computation.50 | loop fusion | flops 2048 | bytes 25156 | tf_op jit(solution)/shard_map/mul | solution.py:91
  45.7 7.8 %all-to-all-done = f32[1,256,128]{2,0,1:T(1,128)S(1)} async-done(((f32[1,256,128]{2,0,1:T(1,128)}), f32[1,256,128]{2,0,1:T(1,128)S(1)}, u32[]{:S(2)}, u32[]{:S(2)}) %all-to-all-start) | async-done | bytes 131104 | tf_op jit(solution)/shard_map/all_to_all | solution.py:95
  53.4 0.4 fusion.4
  53.8 0.7 multiply_convert_fusion.8
  54.6 10.1 %all_to_all.24 = bf16[16,16,128]{2,1,0:T(8,128)(2,1)S(1)} all-to-all(bf16[16,16,128]{2,1,0:T(8,128)(2,1)S(1)} %multiply_convert_fusion.8), channel_id=1, replica_groups=mesh['member'=16,'grid'=32] {'member'}, dimensions={0} | all-to-all | bytes 131072 | tf_op jit(solution)/shard_map/all_to_all | solution.py:103
  64.7 0.4 multiply_reduce_fusion
  65.1 0.0 copy-done.1
  65.1 1.5 %multiply_convert_fusion.5 = bf16[256,1024]{1,0:T(8,128)(2,1)S(1)} fusion(f32[256,1024]{1,0:T(8,128)S(1)} %get-tuple-element.11, f32[256,1024]{1,0:T(8,128)} %copy-done.1, f32[256]{0:T(256)S(1)} %broadcast_multiply_fusion.1, f32[256]{0:T(256)S(1)} %add_rsqrt_fusion), kind=kLoop, calls=%fused_computation.23 | loop fusion | flops 1310720 | bytes 2623488 | tf_op jit(solution)/shard_map/convert_element_type | solution.py:113
  66.6 0.0 copy-start.8
  66.6 0.0 copy-start.10
  66.6 0.0 copy-start.12
  66.6 3.6 %gather_fusion.3 = bf16[768,1024]{1,0:T(8,128)(2,1)} fusion(bf16[256,1024]{1,0:T(8,128)(2,1)S(1)} %multiply_convert_fusion.5, s32[1024]{0:T(1024)S(1)} %pad_clamp_fusion), kind=kCustom, calls=%fused_computation.1.clone | custom fusion | bytes 3148800 | tf_op jit(solution)/shard_map/jit(_take)/gather | solution.py:51
  70.2 0.0 copy-done.8
  70.2 0.0 copy-done.10
  70.2 0.0 copy-done.12
  70.2 0.0 copy-start.6
  70.2 5.9 %multiply_convert_fusion = bf16[768,1024]{1,0:T(8,128)(2,1)} fusion(bf16[1024,1024]{1,0:T(8,128)(2,1)S(1)} %copy-done, bf16[768,1024]{1,0:T(8,128)(2,1)} %gather_fusion.3, pred[768]{0:T(1024)(128)(4,1)S(1)} %copy-done.12, pred[768]{0:T(1024)(128)(4,1)S(1)} %copy-done.10, bf16[768,1024]{1,0:T(8,128)(2,1)} %gather_fusion.2, ...), kind=kOutput, calls=%fused_computation.7 | convolution fusion | flops 1623195648 | bytes 8390912 | tf_op jit(solution)/shard_map/dot_general | solution.py:53
  76.1 9.8 %scatter_custom_fusion = f32[96,1024]{1,0:T(8,128)S(1)} fusion(s32[768]{0:T(1024)} %param.18, bf16[768,1024]{1,0:T(8,128)(2,1)} %multiply_convert_fusion, f32[]{:T(128)} %constant.29.clone.1), kind=kCustom, calls=%fused_computation.5 | custom fusion | flops 1572864 | bytes 1966592 | tf_op jit(solution)/shard_map/scatter-add | solution.py:115
  85.9 0.0 copy-done.6
  85.9 0.2 fusion.29
  86.2 1.9 %collective-permute-start.2 = (bf16[1,48,1024]{2,1,0:T(8,128)(2,1)S(1)}, bf16[1,48,1024]{2,1,0:T(8,128)(2,1)S(1)}, u32[]{:S(2)}, u32[]{:S(2)}) collective-permute-start(bf16[1,48,1024]{2,1,0:T(8,128)(2,1)S(1)} %get-tuple-element.6), channel_id=1, source_target_pairs={{0,1},{1,2},{2,3},{3,4},{4,5},{5,6},{6,7},{7,8},{8,9},{9,10},{10,1... | collective-permute-start | bytes 294920 | tf_op jit(solution)/shard_map/ppermute | solution.py:17
  88.1 7.0 %collective-permute-start.3 = (bf16[1,48,1024]{2,1,0:T(8,128)(2,1)S(1)}, bf16[1,48,1024]{2,1,0:T(8,128)(2,1)S(1)}, u32[]{:S(2)}, u32[]{:S(2)}) collective-permute-start(bf16[1,48,1024]{2,1,0:T(8,128)(2,1)S(1)} %get-tuple-element.7), channel_id=1, source_target_pairs={{1,0},{2,1},{3,2},{4,3},{5,4},{6,5},{7,6},{8,7},{9,8},{10,9},{11,1... | collective-permute-start | bytes 294920 | tf_op jit(solution)/shard_map/ppermute | solution.py:18
  95.1 1.1 %collective-permute-done.2 = bf16[1,48,1024]{2,1,0:T(8,128)(2,1)S(1)} collective-permute-done((bf16[1,48,1024]{2,1,0:T(8,128)(2,1)S(1)}, bf16[1,48,1024]{2,1,0:T(8,128)(2,1)S(1)}, u32[]{:S(2)}, u32[]{:S(2)}) %collective-permute-start.2) | collective-permute-done | bytes 98336 | tf_op jit(solution)/shard_map/ppermute | solution.py:17
  96.1 0.9 collective-permute-done.3
  97.0 0.7 fusion.17
  (10 shorter events, 0.1 us)
Async XLA Ops:
  0.0 30.5 %copy-start = (bf16[1024,1024]{1,0:T(8,128)(2,1)S(1)}, bf16[1024,1024]{1,0:T(8,128)(2,1)}, u32[]{:S(2)}) copy-start(bf16[1024,1024]{1,0:T(8,128)(2,1)} %param.15) | copy-start | bytes 6291460
  0.0 25.9 %collective-permute-start.1 = (bf16[48,1024]{1,0:T(8,128)(2,1)}, bf16[48,1024]{1,0:T(8,128)(2,1)S(1)}, u32[]{:S(2)}, u32[]{:S(2)}) collective-permute-start(bf16[48,1024]{1,0:T(8,128)(2,1)} %bitcast.28), channel_id=1, source_target_pairs={{1,0},{2,1},{3,2},{4,3},{5,4},{6,5},{7,6},{8,7},{9,8},{10,9},{11,1... | collective-permute-start | bytes 294920 | tf_op jit(solution)/shard_map/ppermute | solution.py:18
  13.8 12.1 %collective-permute-start = (bf16[48,1024]{1,0:T(8,128)(2,1)}, bf16[48,1024]{1,0:T(8,128)(2,1)S(1)}, u32[]{:S(2)}, u32[]{:S(2)}) collective-permute-start(bf16[48,1024]{1,0:T(8,128)(2,1)} %bitcast.29), channel_id=1, source_target_pairs={{0,1},{1,2},{2,3},{3,4},{4,5},{5,6},{6,7},{7,8},{8,9},{9,10},{10,1... | collective-permute-start | bytes 294920 | tf_op jit(solution)/shard_map/ppermute | solution.py:17
  16.6 2.1 %copy-start.5 = (s32[96]{0:T(128)}, s32[96]{0:T(128)S(1)}, u32[]{:S(2)}) copy-start(s32[96]{0:T(128)S(1)} %eq.29) | copy-start | bytes 1156
  17.4 13.1 %copy-start.7 = (pred[768]{0:T(1024)(128)(4,1)}, pred[768]{0:T(1024)(128)(4,1)S(1)}, u32[]{:S(2)}) copy-start(pred[768]{0:T(1024)(128)(4,1)S(1)} %compare_and_fusion.1) | copy-start | bytes 2308
  20.2 10.3 %copy-start.9 = (pred[768]{0:T(1024)(128)(4,1)}, pred[768]{0:T(1024)(128)(4,1)S(1)}, u32[]{:S(2)}) copy-start(pred[768]{0:T(1024)(128)(4,1)S(1)} %get-tuple-element.14) | copy-start | bytes 2308
  20.2 10.3 %copy-start.11 = (pred[768]{0:T(1024)(128)(4,1)}, pred[768]{0:T(1024)(128)(4,1)S(1)}, u32[]{:S(2)}) copy-start(pred[768]{0:T(1024)(128)(4,1)S(1)} %get-tuple-element.15) | copy-start | bytes 2308
  20.2 5.7 %copy-start.3 = (bf16[1,48,1024]{2,1,0:T(8,128)(2,1)S(1)}, bf16[1,48,1024]{2,1,0:T(8,128)(2,1)}, u32[]{:S(2)}) copy-start(bf16[1,48,1024]{2,1,0:T(8,128)(2,1)} %param.13) | copy-start | bytes 294916
  26.8 3.6 %copy-start.4 = (s32[768]{0:T(1024)S(1)}, s32[768]{0:T(1024)}, u32[]{:S(2)}) copy-start(s32[768]{0:T(1024)} %param.19) | copy-start | bytes 9220
  30.5 4.7 %copy-start.2 = (bf16[1024,128]{1,0:T(8,128)(2,1)S(1)}, bf16[1024,128]{1,0:T(8,128)(2,1)}, u32[]{:S(2)}) copy-start(bf16[1024,128]{1,0:T(8,128)(2,1)} %param.16) | copy-start | bytes 786436
  30.5 13.8 %copy-start.13 = (f32[256]{0:T(256)S(1)}, f32[256]{0:T(256)}, u32[]{:S(2)}) copy-start(f32[256]{0:T(256)} %param.22) | copy-start | bytes 3076
  35.2 30.0 %copy-start.1 = (f32[256,1024]{1,0:T(8,128)}, f32[256,1024]{1,0:T(8,128)S(1)}, u32[]{:S(2)}) copy-start(f32[256,1024]{1,0:T(8,128)S(1)} %get-tuple-element.9) | copy-start | bytes 3145732
  36.2 17.2 %all-to-all-start = ((f32[1,256,128]{2,0,1:T(1,128)}), f32[1,256,128]{2,0,1:T(1,128)S(1)}, u32[]{:S(2)}, u32[]{:S(2)}) async-start(f32[1,256,128]{2,0,1:T(1,128)} %bitcast.4), calls=%async_computation | async-start | bytes 262144 | tf_op jit(solution)/shard_map/all_to_all | solution.py:95
  66.6 3.6 %copy-start.8 = (pred[768]{0:T(1024)(128)(4,1)S(1)}, pred[768]{0:T(1024)(128)(4,1)}, u32[]{:S(2)}) copy-start(pred[768]{0:T(1024)(128)(4,1)} %copy-done.7) | copy-start | bytes 2308
  66.6 3.6 %copy-start.10 = (pred[768]{0:T(1024)(128)(4,1)S(1)}, pred[768]{0:T(1024)(128)(4,1)}, u32[]{:S(2)}) copy-start(pred[768]{0:T(1024)(128)(4,1)} %copy-done.9) | copy-start | bytes 2308
  66.6 3.6 %copy-start.12 = (pred[768]{0:T(1024)(128)(4,1)S(1)}, pred[768]{0:T(1024)(128)(4,1)}, u32[]{:S(2)}) copy-start(pred[768]{0:T(1024)(128)(4,1)} %copy-done.11) | copy-start | bytes 2308
  70.2 15.7 %copy-start.6 = (s32[96]{0:T(128)S(1)}, s32[96]{0:T(128)}, u32[]{:S(2)}) copy-start(s32[96]{0:T(128)} %copy-done.5) | copy-start | bytes 1156
  86.2 9.9 %collective-permute-start.2 = (bf16[1,48,1024]{2,1,0:T(8,128)(2,1)S(1)}, bf16[1,48,1024]{2,1,0:T(8,128)(2,1)S(1)}, u32[]{:S(2)}, u32[]{:S(2)}) collective-permute-start(bf16[1,48,1024]{2,1,0:T(8,128)(2,1)S(1)} %get-tuple-element.6), channel_id=1, source_target_pairs={{0,1},{1,2},{2,3},{3,4},{4,5},{5,6},{6,7},{7,8},{8,9},{9,10},{10,1... | collective-permute-start | bytes 294920 | tf_op jit(solution)/shard_map/ppermute | solution.py:17
  88.1 8.9 %collective-permute-start.3 = (bf16[1,48,1024]{2,1,0:T(8,128)(2,1)S(1)}, bf16[1,48,1024]{2,1,0:T(8,128)(2,1)S(1)}, u32[]{:S(2)}, u32[]{:S(2)}) collective-permute-start(bf16[1,48,1024]{2,1,0:T(8,128)(2,1)S(1)} %get-tuple-element.7), channel_id=1, source_target_pairs={{1,0},{2,1},{3,2},{4,3},{5,4},{6,5},{7,6},{8,7},{9,8},{10,9},{11,1... | collective-permute-start | bytes 294920 | tf_op jit(solution)/shard_map/ppermute | solution.py:18
where the time goes:
time: 98.4 us; the launch traced here: 97.7 us
  starting transfers between devices  32.7 us (33%)
  other arithmetic  18.1 us (18%)
  local copies, waits for them, and re-layouts  14 us (14%)
  matrix products  12.2 us (12%)
  blocking collectives  10.1 us (10%)
  waiting for transfers between devices  9.7 us (10%)
    ppermute x2, starting transfers between devices, padded(): after = lax.ppermute(initial, axis, down)  20.8 us
    all_to_all x1, blocking collectives, local(): lax.all_to_all(member_grads.astype(jnp.bfloat16), 'member', split_axis=0,...  10.1 us
    scatter-add x1, other arithmetic, local(): jax.ops.segment_sum(grad_pre.astype(jnp.float32), edge_src, num_segments=...  9.77 us
    all_to_all x1, starting transfers between devices, local(): lax.all_to_all(fields[None], 'member', split_axis=1, concat_axis=0, tiled...  8.07 us
    all_to_all x1, waiting for transfers between devices, local(): lax.all_to_all(fields[None], 'member', split_axis=1, concat_axis=0, tiled...  7.78 us
    dot_general x1, matrix products, edge_grads(): lax.dot_general(grad_message, w_msg, (((1,), (1,)), ((), ())), preferred_...  5.91 us
    gather x1, local copies, waits for them, and re-layouts, pre_inputs(): jnp.take(dst_embed, dest_rows, axis=0).astype(jnp.float32)  5.7 us
    dot_general x1, matrix products, spread_points(): jnp.dot(onehot.astype(jnp.bfloat16), message, preferred_element_type=jnp....  4.66 us
  transfers between devices with their start and end apart: 5, of which 3 were waited for; matrix products, arithmetic and copies ran while one was open for 11% of the time, Pallas kernels for 0%

commit v1 on v0

v1 whole, which is shorter than its diff:
```python
import functools

import jax
import jax.numpy as jnp
from jax import lax
from jax.experimental import pallas as pl
from jax.experimental.pallas import tpu as pltpu
from jax.sharding import PartitionSpec as P

smooth_width = 0.1
norm_eps = 1e-06

MESH = pl.DeviceIdType.MESH
NN = (((1,), (0,)), ((), ()))
NT = (((1,), (1,)), ((), ()))
F32 = jnp.float32
BF16 = jnp.bfloat16


def dot(a, b, dims=NN):
    return lax.dot_general(a, b, dims, preferred_element_type=F32)


def onehot(condition):
    return jnp.where(condition, 1.0, 0.0).astype(BF16)


def smooth_slope(gaps):
    return gaps * lax.rsqrt(gaps * gaps + smooth_width * smooth_width)


def sigmoid(v):
    return 0.5 * jnp.tanh(0.5 * v) + 0.5


def body(
    members,
    shards,
    lat_hbm,
    emb_hbm,
    wmsg_hbm,
    wout_hbm,
    need_hbm,
    src_hbm,
    dst_hbm,
    count_hbm,
    target_hbm,
    pw_hbm,
    fw_hbm,
    out_hbm,
    lat,
    emb,
    wmsg,
    wout,
    need,
    src,
    dst,
    count,
    truth,
    pw,
    fw,
    nbr,
    pre,
    od,
    odt,
    n_lr,
    nt,
    summed,
    normed,
    inv,
    fields,
    ens,
    gsend,
    gf,
    w2,
    u,
    rsend,
    own,
    back,
    out,
    pwcol,
    load_sem,
    lat_send,
    lat_recv,
    ens_send,
    ens_recv,
    gf_send,
    gf_recv,
    back_send,
    back_recv,
    out_sem,
):
    node_dev, width = lat.shape
    points = emb.shape[0]
    edges = src.shape[1]
    slots = need.shape[1]
    share = points // members
    chunk = 256
    chunks = width // chunk
    me = lax.axis_index("member")
    g = lax.axis_index("grid")
    left = lax.rem(g + shards - 1, shards)
    right = lax.rem(g + 1, shards)
    rows_me = pl.ds(pl.multiple_of(me * share, share), share)

    def cols(c):
        return pl.ds(c * chunk, chunk)

    loads = []
    for source, target in (
        (src_hbm, src),
        (dst_hbm, dst),
        (need_hbm, need),
        (count_hbm, count),
        (lat_hbm.at[0], lat),
        (emb_hbm, emb),
        (wmsg_hbm, wmsg),
        (wout_hbm, wout),
        (pw_hbm, pw),
        (fw_hbm, fw),
        (target_hbm.at[rows_me], truth),
    ):
        copy = pltpu.make_async_copy(source, target, load_sem.at[len(loads)])
        copy.start()
        loads.append(copy)

    barrier = pltpu.get_barrier_semaphore()
    for neighbour in (left, right):
        pl.semaphore_signal(barrier, inc=1, device_id={"grid": neighbour}, device_id_type=MESH)
    for d in range(1, members):
        pl.semaphore_signal(
            barrier, inc=1, device_id={"member": lax.rem(me + d, members)}, device_id_type=MESH
        )

    for copy in loads[:4]:
        copy.wait()
    lane = lax.broadcasted_iota(jnp.int32, (1, edges), 1)
    dest = jnp.where(lane < count[0], dst[...], -1)
    source = src[...]
    odt[...] = onehot(lax.broadcasted_iota(jnp.int32, (points, edges), 0) == dest)
    dest_col = jnp.transpose(jnp.broadcast_to(dest, (128, edges)))
    lanes = lax.broadcasted_iota(jnp.int32, (edges, 128), 1)
    for first in range(0, points, 128):
        od[:, first : first + 128] = onehot(dest_col == lanes + first)
    os_t = onehot(lax.broadcasted_iota(jnp.int32, (128, edges), 0) == source)
    os_n = onehot(jnp.transpose(jnp.broadcast_to(source, (128, edges))) == lanes)
    code = jnp.concatenate(
        [
            need[0:1, :],
            need[1:2, :] + 2 * node_dev,
            need[2:3, :] + node_dev,
            jnp.full((1, 128 - 3 * slots), -1, jnp.int32),
        ],
        axis=1,
    )
    place = onehot(lax.broadcasted_iota(jnp.int32, (3 * node_dev, 128), 0) == code)
    nt[...] = dot(place, os_t).astype(BF16)
    n_lr[...] = dot(os_n, place[: 2 * node_dev], NT).astype(BF16)
    n_own = dot(os_n, place[2 * node_dev :], NT).astype(BF16)

    loads[4].wait()
    pl.semaphore_wait(barrier, members + 1)
    lat_copies = []
    for c in range(chunks):
        for side, neighbour in ((1, left), (0, right)):
            copy = pltpu.make_async_remote_copy(
                src_ref=lat.at[:, cols(c)],
                dst_ref=nbr.at[pl.ds(side * node_dev, node_dev), cols(c)],
                send_sem=lat_send.at[side, c],
                recv_sem=lat_recv.at[side, c],
                device_id={"grid": neighbour},
                device_id_type=MESH,
            )
            copy.start()
            lat_copies.append(copy)

    loads[5].wait()
    for c in range(chunks):
        pre[:, cols(c)] = dot(od[...], emb[:, cols(c)]) + dot(n_own, lat[:, cols(c)])
    loads[6].wait()
    loads[7].wait()
    w2t = dot(wmsg[...], wout[...])
    high = w2t.astype(BF16)
    w2[:, :128] = high
    w2[:, 128:] = (w2t - high.astype(F32)).astype(BF16)
    for copy in loads[8:]:
        copy.wait()
    pwcol[...] = jnp.transpose(jnp.broadcast_to(pw[...], (128, points)))

    for c in range(chunks):
        for copy in lat_copies[2 * c : 2 * c + 2]:
            copy.wait_recv()
        v = pre[:, cols(c)] + dot(n_lr[...], nbr[:, cols(c)])
        pre[:, cols(c)] = v
        hidden = (v * sigmoid(v)).astype(BF16)
        gathered = dot(odt[...], hidden).astype(BF16)
        part = dot(gathered, wmsg[cols(c), :])
        if c == 0:
            summed[...] = part
        else:
            summed[...] += part
    total = summed[...]
    inv_rms = lax.rsqrt(jnp.mean(total * total, axis=1, keepdims=True) + norm_eps)
    inv[...] = inv_rms
    normed[...] = (total * inv_rms).astype(BF16)
    fields[...] = dot(normed[...], wout[...])

    ens_copies = []
    for d in range(1, members):
        other = lax.rem(me + d, members)
        copy = pltpu.make_async_remote_copy(
            src_ref=fields.at[pl.ds(pl.multiple_of(other * share, share), share)],
            dst_ref=ens.at[d - 1],
            send_sem=ens_send.at[d - 1],
            recv_sem=ens_recv.at[d - 1],
            device_id={"member": other},
            device_id_type=MESH,
        )
        copy.start()
        ens_copies.append(copy)

    for c in range(chunks):
        v = pre[:, cols(c)]
        s = sigmoid(v)
        pre[:, cols(c)] = s * (1.0 + v * (1.0 - s))
    u[...] = dot(normed[...], wmsg[...], NT)

    weights = pwcol[rows_me, :] * fw[...]
    for copy in ens_copies:
        copy.wait_recv()
    x = [fields[rows_me, :]] + [ens[d] for d in range(members - 1)]
    pair = [jnp.zeros_like(x[0]) for _ in x]
    for i in range(members):
        for j in range(i):
            slope = smooth_slope(x[i] - x[j])
            pair[i] = pair[i] + slope
            pair[j] = pair[j] - slope
    y = truth[...]
    grads = [
        (weights * (smooth_slope(x[i] - y) - pair[i] * (1.0 / (members - 1)))).astype(BF16)
        for i in range(members)
    ]
    gf_copies = []
    for d in range(1, members):
        gsend[d - 1] = grads[d]
        copy = pltpu.make_async_remote_copy(
            src_ref=gsend.at[d - 1],
            dst_ref=gf.at[rows_me],
            send_sem=gf_send.at[d - 1],
            recv_sem=gf_recv.at[d - 1],
            device_id={"member": lax.rem(me + members - d, members)},
            device_id_type=MESH,
        )
        copy.start()
        gf_copies.append(copy)
    gf[rows_me, :] = grads[0]
    for copy in gf_copies:
        copy.wait_recv()

    got = gf[...]
    along = jnp.sum(got.astype(F32) * fields[...], axis=1, keepdims=True) * (1.0 / width)
    twice = jnp.concatenate([got, got], axis=1)
    inv_rms = inv[...]
    back_copies = []
    for c in range(chunks):
        grad = inv_rms * (dot(twice, w2[cols(c), :], NT) - along * u[:, cols(c)])
        grad_pre = (dot(od[...], grad.astype(BF16)) * pre[:, cols(c)]).astype(BF16)
        rows = dot(nt[...], grad_pre)
        rsend[:, cols(c)] = rows[: 2 * node_dev].astype(BF16)
        own[:, cols(c)] = rows[2 * node_dev :]
        for side, neighbour in ((0, left), (1, right)):
            copy = pltpu.make_async_remote_copy(
                src_ref=rsend.at[pl.ds(side * node_dev, node_dev), cols(c)],
                dst_ref=back.at[side, :, cols(c)],
                send_sem=back_send.at[side, c],
                recv_sem=back_recv.at[side, c],
                device_id={"grid": neighbour},
                device_id_type=MESH,
            )
            copy.start()
            back_copies.append(copy)
    stores = []
    for c in range(chunks):
        for copy in back_copies[2 * c : 2 * c + 2]:
            copy.wait_recv()
        out[:, cols(c)] = (
            own[:, cols(c)] + back[0, :, cols(c)].astype(F32) + back[1, :, cols(c)].astype(F32)
        )
        copy = pltpu.make_async_copy(out.at[:, cols(c)], out_hbm.at[0, :, cols(c)], out_sem.at[c])
        copy.start()
        stores.append(copy)
    for copy in lat_copies + ens_copies + gf_copies + back_copies:
        copy.wait_send()
    for copy in stores:
        copy.wait()


def local(
    latents,
    dst_embed,
    w_msg,
    w_out,
    need_rows,
    edge_src,
    edge_dst,
    edge_count,
    target,
    point_weight,
    field_weight,
):
    members = lax.axis_size("member")
    shards = lax.axis_size("grid")
    node_dev, width = latents.shape[1:]
    points = dst_embed.shape[0]
    edges = edge_src.shape[0]
    fields = w_out.shape[1]
    share = points // members
    chunks = width // 256
    dma = pltpu.SemaphoreType.DMA
    return pl.pallas_call(
        functools.partial(body, members, shards),
        out_shape=jax.ShapeDtypeStruct((1, node_dev, width), F32),
        in_specs=[pl.BlockSpec(memory_space=pl.ANY)] * 11,
        out_specs=pl.BlockSpec(memory_space=pl.ANY),
        scratch_shapes=[
            pltpu.VMEM((node_dev, width), BF16),
            pltpu.VMEM((points, width), BF16),
            pltpu.VMEM((width, width), BF16),
            pltpu.VMEM((width, fields), BF16),
            pltpu.VMEM(need_rows.shape, jnp.int32),
            pltpu.VMEM((1, edges), jnp.int32),
            pltpu.VMEM((1, edges), jnp.int32),
            pltpu.SMEM((1,), jnp.int32),
            pltpu.VMEM((share, fields), F32),
            pltpu.VMEM((1, points), F32),
            pltpu.VMEM((1, fields), F32),
            pltpu.VMEM((2 * node_dev, width), BF16),
            pltpu.VMEM((edges, width), F32),
            pltpu.VMEM((edges, points), BF16),
            pltpu.VMEM((points, edges), BF16),
            pltpu.VMEM((edges, 2 * node_dev), BF16),
            pltpu.VMEM((3 * node_dev, edges), BF16),
            pltpu.VMEM((points, width), F32),
            pltpu.VMEM((points, width), BF16),
            pltpu.VMEM((points, 1), F32),
            pltpu.VMEM((points, fields), F32),
            pltpu.VMEM((members - 1, share, fields), F32),
            pltpu.VMEM((members - 1, share, fields), BF16),
            pltpu.VMEM((points, fields), BF16),
            pltpu.VMEM((width, 2 * fields), BF16),
            pltpu.VMEM((points, width), F32),
            pltpu.VMEM((2 * node_dev, width), BF16),
            pltpu.VMEM((node_dev, width), F32),
            pltpu.VMEM((2, node_dev, width), BF16),
            pltpu.VMEM((node_dev, width), F32),
            pltpu.VMEM((points, 128), F32),
            dma((11,)),
            dma((2, chunks)),
            dma((2, chunks)),
            dma((members - 1,)),
            dma((members - 1,)),
            dma((members - 1,)),
            dma((members - 1,)),
            dma((2, chunks)),
            dma((2, chunks)),
            dma((chunks,)),
        ],
        compiler_params=pltpu.CompilerParams(
            collective_id=0, has_side_effects=True, vmem_limit_bytes=48 * 1024 * 1024
        ),
        cost_estimate=pl.CostEstimate(
            flops=6_000_000_000, bytes_accessed=4_000_000, transcendentals=1_600_000
        ),
    )(
        latents,
        dst_embed,
        w_msg,
        w_out,
        need_rows,
        edge_src[None],
        edge_dst[None],
        edge_count,
        target,
        point_weight[None],
        field_weight[None],
    )


def solution(mesh):
    placed = (
        P("member", "grid", None),
        P("grid", None),
        P(),
        P(),
        P("grid", None),
        P("grid"),
        P("grid"),
        P("grid"),
        P("grid", None),
        P("grid"),
        P(),
    )
    return jax.shard_map(
        local, mesh=mesh, in_specs=placed, out_specs=P("member", "grid", None), check_vma=False
    )
```

time: 98.4 us -> 51.7 us (0.53)
  Pallas kernels: 0 us -> 41.2 us
  starting transfers between devices: 32.7 us -> 0 us
  other arithmetic: 18.1 us -> 0 us
  matrix products: 12.2 us -> 0 us
  blocking collectives: 10.1 us -> 0 us
  waiting for transfers between devices: 9.7 us -> 0 us
  local copies, waits for them, and re-layouts: 14 us -> 9.45 us
    pallas_call x0 -> x1, Pallas kernels: none -> 41.2 us  [local(): pl.pallas_call(functools.partial(body, members, shards), out_shape=jax.Sh...]
    ppermute x4 -> x0, starting transfers between devices: 24.6 us -> none  [the longest x2 20.8 us: padded(): after = lax.ppermute(initial, axis, down)]
    gather x4 -> x0, local copies, waits for them, and re-layouts: 13.7 us -> none  [the longest x1 5.7 us: pre_inputs(): jnp.take(dst_embed, dest_rows, axis=0).astype(jnp.float32)]
    dot_general x5 -> x0, matrix products: 12.2 us -> none  [the longest x1 5.91 us: edge_grads(): lax.dot_general(grad_message, w_msg, (((1,), (1,)), ((), ())), preferred_...]
    all_to_all x1 -> x0, blocking collectives: 10.1 us -> none  [local(): lax.all_to_all(member_grads.astype(jnp.bfloat16), 'member', split_axis=0,...]
    scatter-add x1 -> x0, other arithmetic: 9.77 us -> none  [local(): jax.ops.segment_sum(grad_pre.astype(jnp.float32), edge_src, num_segments=...]
    all_to_all x1 -> x0, starting transfers between devices: 8.07 us -> none  [local(): lax.all_to_all(fields[None], 'member', split_axis=1, concat_axis=0, tiled...]
    unnamed x28 -> x17, local copies, waits for them, and re-layouts: 0.06 us -> 8.07 us
  transfers between devices with their start and end apart: 5 -> 0, of which waited for: 3 -> 0; matrix products, arithmetic and copies ran while one was open for 11% -> 0% of each run, Pallas kernels for 0% -> 0%
where the time goes in v1:
time: 51.7 us; the launch traced here: 51.4 us
  Pallas kernels  41.2 us (80%)
  local copies, waits for them, and re-layouts  9.45 us (18%)
  between operations  0.67 us (1%)
    pallas_call x1, Pallas kernels, local(): pl.pallas_call(functools.partial(body, members, shards), out_shape=jax.Sh...  41.2 us
    unnamed x17, local copies, waits for them, and re-layouts  8.07 us

profile of v1, /device:TPU:1, one launch (start us, length us, event | category | flops | bytes accessed | tf_op | source)
XLA Modules:
  0.0 51.4 jit_solution(15629164002196759771)
XLA Ops:
  0.7 0.7 %broadcast_in_dim.12.src_hbm = s32[1,768]{1,0:T(1,128)S(1)} reshape(s32[768]{0:T(1024)} %param.16) | data formatting | bytes 6144 | tf_op jit(solution)/shard_map/broadcast_in_dim | solution.py:380
  1.3 0.7 %broadcast_in_dim.13.dst_hbm = s32[1,768]{1,0:T(1,128)S(1)} reshape(s32[768]{0:T(1024)} %param.17) | data formatting | bytes 6144 | tf_op jit(solution)/shard_map/broadcast_in_dim | solution.py:381
  2.0 0.0 copy-start
  2.0 1.6 %copy-done = bf16[1024,1024]{1,0:T(8,128)(2,1)S(1)} copy-done((bf16[1024,1024]{1,0:T(8,128)(2,1)S(1)}, bf16[1024,1024]{1,0:T(8,128)(2,1)}, u32[]{:S(2)}) %copy-start) | copy-done | bytes 2097176
  3.6 0.0 copy-start.1
  3.6 1.0 %copy-done.1 = bf16[256,1024]{1,0:T(8,128)(2,1)S(1)} copy-done((bf16[256,1024]{1,0:T(8,128)(2,1)S(1)}, bf16[256,1024]{1,0:T(8,128)(2,1)}, u32[]{:S(2)}) %copy-start.1) | copy-done | bytes 524312
  4.7 0.0 copy-start.2
  4.7 0.9 %copy-done.2 = bf16[1024,128]{1,0:T(8,128)(2,1)S(1)} copy-done((bf16[1024,128]{1,0:T(8,128)(2,1)S(1)}, bf16[1024,128]{1,0:T(8,128)(2,1)}, u32[]{:S(2)}) %copy-start.2) | copy-done | bytes 262168
  5.6 0.0 copy-start.3
  5.6 0.9 %copy-done.3 = f32[256,128]{1,0:T(8,128)S(1)} copy-done((f32[256,128]{1,0:T(8,128)S(1)}, f32[256,128]{1,0:T(8,128)}, u32[]{:S(2)}) %copy-start.3) | copy-done | bytes 131096
  6.5 0.0 copy-start.4
  6.5 0.9 %copy-done.4 = bf16[1,48,1024]{2,1,0:T(8,128)(2,1)S(1)} copy-done((bf16[1,48,1024]{2,1,0:T(8,128)(2,1)S(1)}, bf16[1,48,1024]{2,1,0:T(8,128)(2,1)}, u32[]{:S(2)}) %copy-start.4) | copy-done | bytes 98328
  7.4 0.0 copy-start.5
  7.4 0.7 %copy-done.5 = s32[3,32]{1,0:T(4,128)S(1)} copy-done((s32[3,32]{1,0:T(4,128)S(1)}, s32[3,32]{1,0:T(4,128)}, u32[]{:S(2)}) %copy-start.5) | copy-done | bytes 408
  8.1 0.0 copy-start.6
  8.1 0.7 %copy-done.6 = f32[256]{0:T(256)S(1)} copy-done((f32[256]{0:T(256)S(1)}, f32[256]{0:T(256)}, u32[]{:S(2)}) %copy-start.6) | copy-done | bytes 1048
  8.8 0.0 copy-start.7
  8.8 0.7 %copy-done.7 = f32[128]{0:T(128)S(1)} copy-done((f32[128]{0:T(128)S(1)}, f32[128]{0:T(128)}, u32[]{:S(2)}) %copy-start.7) | copy-done | bytes 536
  9.4 41.2 %shard_map.109 = f32[1,48,1024]{2,1,0:T(8,128)S(1)} custom-call(bf16[1,48,1024]{2,1,0:T(8,128)(2,1)S(1)} %copy-done.4, bf16[256,1024]{1,0:T(8,128)(2,1)S(1)} %copy-done.1, bf16[1024,1024]{1,0:T(8,128)(2,1)S(1)} %copy-done, bf16[1024,128]{1,0:T(8,128)(2,1)S(1)} %copy-done.2, s32[3,32]{1,0:T(4,128)S(1)} %copy-done.5, s32[1,768]{1,0:T(1,128)S(1)} %broadcast_in_dim.12.src_hbm, ...), custom_call_target="tpu_custom_call" | custom-call | flops 6000000000 | bytes 4000000 | tf_op jit(solution)/shard_map/pallas_call | solution.py:320
  50.7 0.7 %copy.14 = f32[1,48,1024]{2,1,0:T(8,128)} copy(f32[1,48,1024]{2,1,0:T(8,128)S(1)} %shard_map.109) | data formatting | bytes 393216
Async XLA Ops:
  2.0 1.6 %copy-start = (bf16[1024,1024]{1,0:T(8,128)(2,1)S(1)}, bf16[1024,1024]{1,0:T(8,128)(2,1)}, u32[]{:S(2)}) copy-start(bf16[1024,1024]{1,0:T(8,128)(2,1)} %wmsg_hbm.1) | copy-start | bytes 6291460
  3.6 1.0 %copy-start.1 = (bf16[256,1024]{1,0:T(8,128)(2,1)S(1)}, bf16[256,1024]{1,0:T(8,128)(2,1)}, u32[]{:S(2)}) copy-start(bf16[256,1024]{1,0:T(8,128)(2,1)} %emb_hbm.1) | copy-start | bytes 1572868
  4.7 0.9 %copy-start.2 = (bf16[1024,128]{1,0:T(8,128)(2,1)S(1)}, bf16[1024,128]{1,0:T(8,128)(2,1)}, u32[]{:S(2)}) copy-start(bf16[1024,128]{1,0:T(8,128)(2,1)} %wout_hbm.1) | copy-start | bytes 786436
  5.6 0.9 %copy-start.3 = (f32[256,128]{1,0:T(8,128)S(1)}, f32[256,128]{1,0:T(8,128)}, u32[]{:S(2)}) copy-start(f32[256,128]{1,0:T(8,128)} %target_hbm.1) | copy-start | bytes 393220
  6.5 0.9 %copy-start.4 = (bf16[1,48,1024]{2,1,0:T(8,128)(2,1)S(1)}, bf16[1,48,1024]{2,1,0:T(8,128)(2,1)}, u32[]{:S(2)}) copy-start(bf16[1,48,1024]{2,1,0:T(8,128)(2,1)} %lat_hbm.1) | copy-start | bytes 294916
  7.4 0.7 %copy-start.5 = (s32[3,32]{1,0:T(4,128)S(1)}, s32[3,32]{1,0:T(4,128)}, u32[]{:S(2)}) copy-start(s32[3,32]{1,0:T(4,128)} %need_hbm.1) | copy-start | bytes 1156
  8.1 0.7 %copy-start.6 = (f32[256]{0:T(256)S(1)}, f32[256]{0:T(256)}, u32[]{:S(2)}) copy-start(f32[256]{0:T(256)} %param.20) | copy-start | bytes 3076
  8.8 0.7 %copy-start.7 = (f32[128]{0:T(128)S(1)}, f32[128]{0:T(128)}, u32[]{:S(2)}) copy-start(f32[128]{0:T(128)} %param.21) | copy-start | bytes 1540

commit v2 on v1

--- a/solution.py
+++ b/solution.py
@@ -47,7 +47,7 @@
     target_hbm,
     pw_hbm,
     fw_hbm,
-    out_hbm,
+    out,
     lat,
     emb,
     wmsg,
@@ -77,7 +77,6 @@
     rsend,
     own,
     back,
-    out,
     pwcol,
     load_sem,
     lat_send,
@@ -88,11 +87,10 @@
     gf_recv,
     back_send,
     back_recv,
-    out_sem,
 ):
     node_dev, width = lat.shape
     points = emb.shape[0]
-    edges = src.shape[1]
+    edges = src.shape[0]
     slots = need.shape[1]
     share = points // members
     chunk = 256
@@ -103,8 +101,18 @@
     right = lax.rem(g + 1, shards)
     rows_me = pl.ds(pl.multiple_of(me * share, share), share)
 
+    order = sorted(range(1, members), key=lambda d: -min(d, members - d))
+
     def cols(c):
         return pl.ds(c * chunk, chunk)
+
+    barrier = pltpu.get_barrier_semaphore()
+    for neighbour in (left, right):
+        pl.semaphore_signal(barrier, inc=1, device_id={"grid": neighbour}, device_id_type=MESH)
+    for d in order:
+        pl.semaphore_signal(
+            barrier, inc=1, device_id={"member": lax.rem(me + d, members)}, device_id_type=MESH
+        )
 
     loads = []
     for source, target in (
@@ -124,19 +132,11 @@
         copy.start()
         loads.append(copy)
 
-    barrier = pltpu.get_barrier_semaphore()
-    for neighbour in (left, right):
-        pl.semaphore_signal(barrier, inc=1, device_id={"grid": neighbour}, device_id_type=MESH)
-    for d in range(1, members):
-        pl.semaphore_signal(
-            barrier, inc=1, device_id={"member": lax.rem(me + d, members)}, device_id_type=MESH
-        )
-
     for copy in loads[:4]:
         copy.wait()
     lane = lax.broadcasted_iota(jnp.int32, (1, edges), 1)
-    dest = jnp.where(lane < count[0], dst[...], -1)
-    source = src[...]
+    dest = jnp.where(lane < count[0], dst[...].reshape(1, edges), -1)
+    source = src[...].reshape(1, edges)
     odt[...] = onehot(lax.broadcasted_iota(jnp.int32, (points, edges), 0) == dest)
     dest_col = jnp.transpose(jnp.broadcast_to(dest, (128, edges)))
     lanes = lax.broadcasted_iota(jnp.int32, (edges, 128), 1)
@@ -185,7 +185,7 @@
     w2[:, 128:] = (w2t - high.astype(F32)).astype(BF16)
     for copy in loads[8:]:
         copy.wait()
-    pwcol[...] = jnp.transpose(jnp.broadcast_to(pw[...], (128, points)))
+    pwcol[...] = jnp.transpose(jnp.broadcast_to(pw[...].reshape(1, points), (128, points)))
 
     for c in range(chunks):
         for copy in lat_copies[2 * c : 2 * c + 2]:
@@ -206,7 +206,7 @@
     fields[...] = dot(normed[...], wout[...])
 
     ens_copies = []
-    for d in range(1, members):
+    for d in order:
         other = lax.rem(me + d, members)
         copy = pltpu.make_async_remote_copy(
             src_ref=fields.at[pl.ds(pl.multiple_of(other * share, share), share)],
@@ -225,7 +225,7 @@
         pre[:, cols(c)] = s * (1.0 + v * (1.0 - s))
     u[...] = dot(normed[...], wmsg[...], NT)
 
-    weights = pwcol[rows_me, :] * fw[...]
+    weights = pwcol[rows_me, :] * fw[...].reshape(1, fw.shape[0])
     for copy in ens_copies:
         copy.wait_recv()
     x = [fields[rows_me, :]] + [ens[d] for d in range(members - 1)]
@@ -241,7 +241,7 @@
         for i in range(members)
     ]
     gf_copies = []
-    for d in range(1, members):
+    for d in order:
         gsend[d - 1] = grads[d]
         copy = pltpu.make_async_remote_copy(
             src_ref=gsend.at[d - 1],
@@ -279,20 +279,14 @@
             )
             copy.start()
             back_copies.append(copy)
-    stores = []
     for c in range(chunks):
         for copy in back_copies[2 * c : 2 * c + 2]:
             copy.wait_recv()
-        out[:, cols(c)] = (
+        out[0, :, cols(c)] = (
             own[:, cols(c)] + back[0, :, cols(c)].astype(F32) + back[1, :, cols(c)].astype(F32)
         )
-        copy = pltpu.make_async_copy(out.at[:, cols(c)], out_hbm.at[0, :, cols(c)], out_sem.at[c])
-        copy.start()
-        stores.append(copy)
     for copy in lat_copies + ens_copies + gf_copies + back_copies:
         copy.wait_send()
-    for copy in stores:
-        copy.wait()
 
 
 def local(
@@ -319,21 +313,21 @@
     dma = pltpu.SemaphoreType.DMA
     return pl.pallas_call(
         functools.partial(body, members, shards),
-        out_shape=jax.ShapeDtypeStruct((1, node_dev, width), F32),
+        out_shape=pltpu.VMEM((1, node_dev, width), F32),
         in_specs=[pl.BlockSpec(memory_space=pl.ANY)] * 11,
-        out_specs=pl.BlockSpec(memory_space=pl.ANY),
+        out_specs=pl.BlockSpec(memory_space=pltpu.VMEM),
         scratch_shapes=[
             pltpu.VMEM((node_dev, width), BF16),
             pltpu.VMEM((points, width), BF16),
             pltpu.VMEM((width, width), BF16),
             pltpu.VMEM((width, fields), BF16),
             pltpu.VMEM(need_rows.shape, jnp.int32),
-            pltpu.VMEM((1, edges), jnp.int32),
-            pltpu.VMEM((1, edges), jnp.int32),
+            pltpu.VMEM((edges,), jnp.int32),
+            pltpu.VMEM((edges,), jnp.int32),
             pltpu.SMEM((1,), jnp.int32),
             pltpu.VMEM((share, fields), F32),
-            pltpu.VMEM((1, points), F32),
-            pltpu.VMEM((1, fields), F32),
+            pltpu.VMEM((points,), F32),
+            pltpu.VMEM((fields,), F32),
             pltpu.VMEM((2 * node_dev, width), BF16),
             pltpu.VMEM((edges, width), F32),
             pltpu.VMEM((edges, points), BF16),
@@ -352,7 +346,6 @@
             pltpu.VMEM((2 * node_dev, width), BF16),
             pltpu.VMEM((node_dev, width), F32),
             pltpu.VMEM((2, node_dev, width), BF16),
-            pltpu.VMEM((node_dev, width), F32),
             pltpu.VMEM((points, 128), F32),
             dma((11,)),
             dma((2, chunks)),
@@ -363,26 +356,25 @@
             dma((members - 1,)),
             dma((2, chunks)),
             dma((2, chunks)),
-            dma((chunks,)),
         ],
         compiler_params=pltpu.CompilerParams(
-            collective_id=0, has_side_effects=True, vmem_limit_bytes=48 * 1024 * 1024
+            collective_id=0, has_side_effects=True, vmem_limit_bytes=32 * 1024 * 1024
         ),
         cost_estimate=pl.CostEstimate(
             flops=6_000_000_000, bytes_accessed=4_000_000, transcendentals=1_600_000
         ),
     )(
-        latents,
-        dst_embed,
-        w_msg,
-        w_out,
-        need_rows,
-        edge_src[None],
-        edge_dst[None],
+        pltpu.with_memory_space_constraint(latents, pltpu.HBM),
+        pltpu.with_memory_space_constraint(dst_embed, pltpu.HBM),
+        pltpu.with_memory_space_constraint(w_msg, pltpu.HBM),
+        pltpu.with_memory_space_constraint(w_out, pltpu.HBM),
+        pltpu.with_memory_space_constraint(need_rows, pltpu.HBM),
+        pltpu.with_memory_space_constraint(edge_src, pltpu.HBM),
+        pltpu.with_memory_space_constraint(edge_dst, pltpu.HBM),
         edge_count,
-        target,
-        point_weight[None],
-        field_weight[None],
+        pltpu.with_memory_space_constraint(target, pltpu.HBM),
+        pltpu.with_memory_space_constraint(point_weight, pltpu.HBM),
+        pltpu.with_memory_space_constraint(field_weight, pltpu.HBM),
     )
 
 

time: 51.7 us -> 41.8 us (0.81)
  local copies, waits for them, and re-layouts: 9.45 us -> 0.68 us
  Pallas kernels: 41.2 us -> 40.4 us
    unnamed x17 -> x1, local copies, waits for them, and re-layouts: 8.07 us -> 0.68 us
    broadcast_in_dim x2 -> x0, local copies, waits for them, and re-layouts: 1.38 us -> none  [the longest x1 0.69 us: local(): edge_src[None]]
    pallas_call x1, Pallas kernels: 41.2 us -> 40.4 us  [local(): pl.pallas_call(functools.partial(body, members, shards), out_shape=pltpu....]
where the time goes in v2:
time: 41.8 us; the launch traced here: 41.7 us
  Pallas kernels  40.4 us (97%)
  local copies, waits for them, and re-layouts  0.68 us (2%)
  between operations  0.66 us (2%)
    pallas_call x1, Pallas kernels, local(): pl.pallas_call(functools.partial(body, members, shards), out_shape=pltpu....  40.4 us

profile of v2, /device:TPU:1, one launch (start us, length us, event | category | flops | bytes accessed | tf_op | source)
XLA Modules:
  0.0 41.7 jit_solution(11726795710890022070)
XLA Ops:
  0.7 40.4 %shard_map.109 = f32[1,48,1024]{2,1,0:T(8,128)S(1)} custom-call(bf16[1,48,1024]{2,1,0:T(8,128)(2,1)} %lat_hbm.1, bf16[256,1024]{1,0:T(8,128)(2,1)} %emb_hbm.1, bf16[1024,1024]{1,0:T(8,128)(2,1)} %wmsg_hbm.1, bf16[1024,128]{1,0:T(8,128)(2,1)} %wout_hbm.1, s32[3,32]{1,0:T(4,128)} %need_hbm.1, s32[768]{0:T(1024)} %src_hbm.1, s32[768]{0:T(1024)} %dst_hbm.1, ...), custom_call_target="tpu_custom_call" | custom-call | flops 6000000000 | bytes 4000000 | tf_op jit(solution)/shard_map/pallas_call | solution.py:314
  41.0 0.7 %copy.13 = f32[1,48,1024]{2,1,0:T(8,128)} copy(f32[1,48,1024]{2,1,0:T(8,128)S(1)} %shard_map.109) | data formatting | bytes 393216

commit v3 on v2

--- a/solution.py
+++ b/solution.py
@@ -66,7 +66,7 @@
     n_lr,
     nt,
     summed,
-    normed,
+    total16,
     inv,
     fields,
     ens,
@@ -74,6 +74,7 @@
     gf,
     w2,
     u,
+    grad,
     rsend,
     own,
     back,
@@ -87,6 +88,7 @@
     gf_recv,
     back_send,
     back_recv,
+    relay,
 ):
     node_dev, width = lat.shape
     points = emb.shape[0]
@@ -103,16 +105,18 @@
 
     order = sorted(range(1, members), key=lambda d: -min(d, members - d))
 
+    def ring(d):
+        return lax.rem(me + members + d, members)
+
     def cols(c):
         return pl.ds(c * chunk, chunk)
 
     barrier = pltpu.get_barrier_semaphore()
     for neighbour in (left, right):
         pl.semaphore_signal(barrier, inc=1, device_id={"grid": neighbour}, device_id_type=MESH)
-    for d in order:
-        pl.semaphore_signal(
-            barrier, inc=1, device_id={"member": lax.rem(me + d, members)}, device_id_type=MESH
-        )
+    mate = me + 1 - 2 * lax.rem(me, 2)
+    for other in (mate, ring(2), ring(-2)):
+        pl.semaphore_signal(barrier, inc=1, device_id={"member": other}, device_id_type=MESH)
 
     loads = []
     for source, target in (
@@ -159,7 +163,7 @@
     n_own = dot(os_n, place[2 * node_dev :], NT).astype(BF16)
 
     loads[4].wait()
-    pl.semaphore_wait(barrier, members + 1)
+    pl.semaphore_wait(barrier, 5)
     lat_copies = []
     for c in range(chunks):
         for side, neighbour in ((1, left), (0, right)):
@@ -174,18 +178,26 @@
             copy.start()
             lat_copies.append(copy)
 
+    for other in (ring(2), ring(-2)):
+        pl.semaphore_signal(relay.at[0], inc=1, device_id={"member": other}, device_id_type=MESH)
     loads[5].wait()
     for c in range(chunks):
         pre[:, cols(c)] = dot(od[...], emb[:, cols(c)]) + dot(n_own, lat[:, cols(c)])
+    pl.semaphore_wait(relay.at[0], 2)
+    for other in (ring(4), ring(-4)):
+        pl.semaphore_signal(relay.at[1], inc=1, device_id={"member": other}, device_id_type=MESH)
     loads[6].wait()
     loads[7].wait()
-    w2t = dot(wmsg[...], wout[...])
-    high = w2t.astype(BF16)
-    w2[:, :128] = high
-    w2[:, 128:] = (w2t - high.astype(F32)).astype(BF16)
+    product = jnp.transpose(dot(wmsg[...], wout[...]))
+    high = product.astype(BF16)
+    w2[: high.shape[0], :] = high
+    w2[high.shape[0] :, :] = (product - high.astype(F32)).astype(BF16)
     for copy in loads[8:]:
         copy.wait()
     pwcol[...] = jnp.transpose(jnp.broadcast_to(pw[...].reshape(1, points), (128, points)))
+
+    pl.semaphore_wait(relay.at[1], 2)
+    pl.semaphore_signal(relay.at[2], inc=1, device_id={"member": mate}, device_id_type=MESH)
 
     for c in range(chunks):
         for copy in lat_copies[2 * c : 2 * c + 2]:
@@ -200,11 +212,12 @@
         else:
             summed[...] += part
     total = summed[...]
+    total16[...] = total.astype(BF16)
     inv_rms = lax.rsqrt(jnp.mean(total * total, axis=1, keepdims=True) + norm_eps)
+    fields[...] = dot(total16[...], wout[...]) * inv_rms
     inv[...] = inv_rms
-    normed[...] = (total * inv_rms).astype(BF16)
-    fields[...] = dot(normed[...], wout[...])
-
+
+    pl.semaphore_wait(relay.at[2], 1)
     ens_copies = []
     for d in order:
         other = lax.rem(me + d, members)
@@ -223,7 +236,8 @@
         v = pre[:, cols(c)]
         s = sigmoid(v)
         pre[:, cols(c)] = s * (1.0 + v * (1.0 - s))
-    u[...] = dot(normed[...], wmsg[...], NT)
+    inv_rms = inv[...]
+    u[...] = dot(total16[...], wmsg[...], NT) * (inv_rms * inv_rms)
 
     weights = pwcol[rows_me, :] * fw[...].reshape(1, fw.shape[0])
     for copy in ens_copies:
@@ -261,10 +275,14 @@
     along = jnp.sum(got.astype(F32) * fields[...], axis=1, keepdims=True) * (1.0 / width)
     twice = jnp.concatenate([got, got], axis=1)
     inv_rms = inv[...]
+    grad[...] = (inv_rms * dot(twice, w2[...]) - along * u[...]).astype(BF16)
     back_copies = []
-    for c in range(chunks):
-        grad = inv_rms * (dot(twice, w2[cols(c), :], NT) - along * u[:, cols(c)])
-        grad_pre = (dot(od[...], grad.astype(BF16)) * pre[:, cols(c)]).astype(BF16)
+    ahead = dot(od[...], grad[:, cols(0)])
+    for c in range(chunks):
+        spread = ahead
+        if c + 1 < chunks:
+            ahead = dot(od[...], grad[:, cols(c + 1)])
+        grad_pre = (spread * pre[:, cols(c)]).astype(BF16)
         rows = dot(nt[...], grad_pre)
         rsend[:, cols(c)] = rows[: 2 * node_dev].astype(BF16)
         own[:, cols(c)] = rows[2 * node_dev :]
@@ -341,8 +359,9 @@
             pltpu.VMEM((members - 1, share, fields), F32),
             pltpu.VMEM((members - 1, share, fields), BF16),
             pltpu.VMEM((points, fields), BF16),
-            pltpu.VMEM((width, 2 * fields), BF16),
+            pltpu.VMEM((2 * fields, width), BF16),
             pltpu.VMEM((points, width), F32),
+            pltpu.VMEM((points, width), BF16),
             pltpu.VMEM((2 * node_dev, width), BF16),
             pltpu.VMEM((node_dev, width), F32),
             pltpu.VMEM((2, node_dev, width), BF16),
@@ -356,6 +375,7 @@
             dma((members - 1,)),
             dma((2, chunks)),
             dma((2, chunks)),
+            pltpu.SemaphoreType.REGULAR((3,)),
         ],
         compiler_params=pltpu.CompilerParams(
             collective_id=0, has_side_effects=True, vmem_limit_bytes=32 * 1024 * 1024

time: 41.8 us -> 40.8 us (0.976)
  Pallas kernels: 40.4 us -> 39.3 us
    pallas_call x1, Pallas kernels: 40.4 us -> 39.3 us  [local(): pl.pallas_call(functools.partial(body, members, shards), out_shape=pltpu....]
where the time goes in v3:
time: 40.8 us; the launch traced here: 40.7 us
  Pallas kernels  39.3 us (96%)
  local copies, waits for them, and re-layouts  0.68 us (2%)
  between operations  0.66 us (2%)
    pallas_call x1, Pallas kernels, local(): pl.pallas_call(functools.partial(body, members, shards), out_shape=pltpu....  39.3 us

profile of v3, /device:TPU:1, one launch (start us, length us, event | category | flops | bytes accessed | tf_op | source)
XLA Modules:
  0.0 40.7 jit_solution(16548097084602320262)
XLA Ops:
  0.7 39.3 %shard_map.109 = f32[1,48,1024]{2,1,0:T(8,128)S(1)} custom-call(bf16[1,48,1024]{2,1,0:T(8,128)(2,1)} %lat_hbm.1, bf16[256,1024]{1,0:T(8,128)(2,1)} %emb_hbm.1, bf16[1024,1024]{1,0:T(8,128)(2,1)} %wmsg_hbm.1, bf16[1024,128]{1,0:T(8,128)(2,1)} %wout_hbm.1, s32[3,32]{1,0:T(4,128)} %need_hbm.1, s32[768]{0:T(1024)} %src_hbm.1, s32[768]{0:T(1024)} %dst_hbm.1, ...), custom_call_target="tpu_custom_call" | custom-call | flops 6000000000 | bytes 4000000 | tf_op jit(solution)/shard_map/pallas_call | solution.py:332
  40.0 0.7 %copy.13 = f32[1,48,1024]{2,1,0:T(8,128)} copy(f32[1,48,1024]{2,1,0:T(8,128)S(1)} %shard_map.109) | data formatting | bytes 393216

commit v4 on v3

--- a/solution.py
+++ b/solution.py
@@ -65,16 +65,17 @@
     odt,
     n_lr,
     nt,
+    gathered,
     summed,
     total16,
     inv,
     fields,
     ens,
+    fields16,
     gsend,
     gf,
     w2,
     u,
-    grad,
     rsend,
     own,
     back,
@@ -105,6 +106,9 @@
 
     order = sorted(range(1, members), key=lambda d: -min(d, members - d))
 
+    def arrived(block, sem):
+        pltpu.make_async_copy(block, block, sem).wait()
+
     def ring(d):
         return lax.rem(me + members + d, members)
 
@@ -165,18 +169,17 @@
     loads[4].wait()
     pl.semaphore_wait(barrier, 5)
     lat_copies = []
-    for c in range(chunks):
-        for side, neighbour in ((1, left), (0, right)):
-            copy = pltpu.make_async_remote_copy(
-                src_ref=lat.at[:, cols(c)],
-                dst_ref=nbr.at[pl.ds(side * node_dev, node_dev), cols(c)],
-                send_sem=lat_send.at[side, c],
-                recv_sem=lat_recv.at[side, c],
-                device_id={"grid": neighbour},
-                device_id_type=MESH,
-            )
-            copy.start()
-            lat_copies.append(copy)
+    for side, neighbour in ((1, left), (0, right)):
+        copy = pltpu.make_async_remote_copy(
+            src_ref=lat,
+            dst_ref=nbr.at[pl.ds(side * node_dev, node_dev)],
+            send_sem=lat_send.at[side],
+            recv_sem=lat_recv.at[side],
+            device_id={"grid": neighbour},
+            device_id_type=MESH,
+        )
+        copy.start()
+        lat_copies.append(copy)
 
     for other in (ring(2), ring(-2)):
         pl.semaphore_signal(relay.at[0], inc=1, device_id={"member": other}, device_id_type=MESH)
@@ -188,6 +191,47 @@
         pl.semaphore_signal(relay.at[1], inc=1, device_id={"member": other}, device_id_type=MESH)
     loads[6].wait()
     loads[7].wait()
+    pl.semaphore_wait(relay.at[1], 2)
+    pl.semaphore_signal(relay.at[2], inc=1, device_id={"member": mate}, device_id_type=MESH)
+
+    def hidden(c):
+        v = pre[:, cols(c)] + dot(n_lr[...], nbr[:, cols(c)])
+        pre[:, cols(c)] = v
+        return (v * sigmoid(v)).astype(BF16)
+
+    for copy in lat_copies:
+        copy.wait_recv()
+    ahead = hidden(0)
+    for c in range(chunks - 1):
+        now = ahead
+        ahead = hidden(c + 1)
+        gathered[:, cols(c)] = dot(odt[...], now).astype(BF16)
+    gathered[:, cols(chunks - 1)] = dot(odt[...], ahead).astype(BF16)
+    total = dot(gathered[...], wmsg[...])
+    total16[...] = total.astype(BF16)
+    inv_rms = lax.rsqrt(jnp.mean(total * total, axis=1, keepdims=True) + norm_eps)
+    fields[...] = dot(total16[...], wout[...]) * inv_rms
+    inv[...] = inv_rms
+
+    pl.semaphore_wait(relay.at[2], 1)
+    fields16[...] = fields[...].astype(BF16)
+    for d in order:
+        other = lax.rem(me + d, members)
+        copy = pltpu.make_async_remote_copy(
+            src_ref=fields16.at[pl.ds(pl.multiple_of(other * share, share), share)],
+            dst_ref=ens.at[d - 1],
+            send_sem=ens_send,
+            recv_sem=ens_recv,
+            device_id={"member": other},
+            device_id_type=MESH,
+        )
+        copy.start()
+
+    for c in range(chunks):
+        v = pre[:, cols(c)]
+        s = sigmoid(v)
+        pre[:, cols(c)] = s * (1.0 + v * (1.0 - s))
+    inv_rms = inv[...]
     product = jnp.transpose(dot(wmsg[...], wout[...]))
     high = product.astype(BF16)
     w2[: high.shape[0], :] = high
@@ -196,53 +240,13 @@
         copy.wait()
     pwcol[...] = jnp.transpose(jnp.broadcast_to(pw[...].reshape(1, points), (128, points)))
 
-    pl.semaphore_wait(relay.at[1], 2)
-    pl.semaphore_signal(relay.at[2], inc=1, device_id={"member": mate}, device_id_type=MESH)
-
-    for c in range(chunks):
-        for copy in lat_copies[2 * c : 2 * c + 2]:
-            copy.wait_recv()
-        v = pre[:, cols(c)] + dot(n_lr[...], nbr[:, cols(c)])
-        pre[:, cols(c)] = v
-        hidden = (v * sigmoid(v)).astype(BF16)
-        gathered = dot(odt[...], hidden).astype(BF16)
-        part = dot(gathered, wmsg[cols(c), :])
-        if c == 0:
-            summed[...] = part
-        else:
-            summed[...] += part
-    total = summed[...]
-    total16[...] = total.astype(BF16)
-    inv_rms = lax.rsqrt(jnp.mean(total * total, axis=1, keepdims=True) + norm_eps)
-    fields[...] = dot(total16[...], wout[...]) * inv_rms
-    inv[...] = inv_rms
-
-    pl.semaphore_wait(relay.at[2], 1)
-    ens_copies = []
-    for d in order:
-        other = lax.rem(me + d, members)
-        copy = pltpu.make_async_remote_copy(
-            src_ref=fields.at[pl.ds(pl.multiple_of(other * share, share), share)],
-            dst_ref=ens.at[d - 1],
-            send_sem=ens_send.at[d - 1],
-            recv_sem=ens_recv.at[d - 1],
-            device_id={"member": other},
-            device_id_type=MESH,
-        )
-        copy.start()
-        ens_copies.append(copy)
-
-    for c in range(chunks):
-        v = pre[:, cols(c)]
-        s = sigmoid(v)
-        pre[:, cols(c)] = s * (1.0 + v * (1.0 - s))
-    inv_rms = inv[...]
     u[...] = dot(total16[...], wmsg[...], NT) * (inv_rms * inv_rms)
 
     weights = pwcol[rows_me, :] * fw[...].reshape(1, fw.shape[0])
-    for copy in ens_copies:
-        copy.wait_recv()
-    x = [fields[rows_me, :]] + [ens[d] for d in range(members - 1)]
+    for copy in lat_copies:
+        copy.wait_send()
+    arrived(ens, ens_recv)
+    x = [fields16[rows_me, :].astype(F32)] + [ens[d].astype(F32) for d in range(members - 1)]
     pair = [jnp.zeros_like(x[0]) for _ in x]
     for i in range(members):
         for j in range(i):
@@ -254,34 +258,38 @@
         (weights * (smooth_slope(x[i] - y) - pair[i] * (1.0 / (members - 1)))).astype(BF16)
         for i in range(members)
     ]
-    gf_copies = []
     for d in order:
         gsend[d - 1] = grads[d]
         copy = pltpu.make_async_remote_copy(
             src_ref=gsend.at[d - 1],
             dst_ref=gf.at[rows_me],
-            send_sem=gf_send.at[d - 1],
-            recv_sem=gf_recv.at[d - 1],
+            send_sem=gf_send,
+            recv_sem=gf_recv,
             device_id={"member": lax.rem(me + members - d, members)},
             device_id_type=MESH,
         )
         copy.start()
-        gf_copies.append(copy)
     gf[rows_me, :] = grads[0]
-    for copy in gf_copies:
-        copy.wait_recv()
+    arrived(ens, ens_send)
+    arrived(gsend, gf_recv)
 
     got = gf[...]
     along = jnp.sum(got.astype(F32) * fields[...], axis=1, keepdims=True) * (1.0 / width)
     twice = jnp.concatenate([got, got], axis=1)
     inv_rms = inv[...]
-    grad[...] = (inv_rms * dot(twice, w2[...]) - along * u[...]).astype(BF16)
+
+    def point_grads(c):
+        return (inv_rms * dot(twice, w2[:, cols(c)]) - along * u[:, cols(c)]).astype(BF16)
+
     back_copies = []
-    ahead = dot(od[...], grad[:, cols(0)])
+    ahead = dot(od[...], point_grads(0))
+    grad = point_grads(1)
     for c in range(chunks):
         spread = ahead
         if c + 1 < chunks:
-            ahead = dot(od[...], grad[:, cols(c + 1)])
+            ahead = dot(od[...], grad)
+        if c + 2 < chunks:
+            grad = point_grads(c + 2)
         grad_pre = (spread * pre[:, cols(c)]).astype(BF16)
         rows = dot(nt[...], grad_pre)
         rsend[:, cols(c)] = rows[: 2 * node_dev].astype(BF16)
@@ -297,13 +305,14 @@
             )
             copy.start()
             back_copies.append(copy)
+    arrived(gsend, gf_send)
     for c in range(chunks):
         for copy in back_copies[2 * c : 2 * c + 2]:
             copy.wait_recv()
         out[0, :, cols(c)] = (
             own[:, cols(c)] + back[0, :, cols(c)].astype(F32) + back[1, :, cols(c)].astype(F32)
         )
-    for copy in lat_copies + ens_copies + gf_copies + back_copies:
+    for copy in back_copies:
         copy.wait_send()
 
 
@@ -352,27 +361,28 @@
             pltpu.VMEM((points, edges), BF16),
             pltpu.VMEM((edges, 2 * node_dev), BF16),
             pltpu.VMEM((3 * node_dev, edges), BF16),
+            pltpu.VMEM((points, width), BF16),
             pltpu.VMEM((points, width), F32),
             pltpu.VMEM((points, width), BF16),
             pltpu.VMEM((points, 1), F32),
             pltpu.VMEM((points, fields), F32),
-            pltpu.VMEM((members - 1, share, fields), F32),
+            pltpu.VMEM((members - 1, share, fields), BF16),
+            pltpu.VMEM((points, fields), BF16),
             pltpu.VMEM((members - 1, share, fields), BF16),
             pltpu.VMEM((points, fields), BF16),
             pltpu.VMEM((2 * fields, width), BF16),
             pltpu.VMEM((points, width), F32),
-            pltpu.VMEM((points, width), BF16),
             pltpu.VMEM((2 * node_dev, width), BF16),
             pltpu.VMEM((node_dev, width), F32),
             pltpu.VMEM((2, node_dev, width), BF16),
             pltpu.VMEM((points, 128), F32),
             dma((11,)),
-            dma((2, chunks)),
-            dma((2, chunks)),
-            dma((members - 1,)),
-            dma((members - 1,)),
-            dma((members - 1,)),
-            dma((members - 1,)),
+            dma((2,)),
+            dma((2,)),
+            dma,
+            dma,
+            dma,
+            dma,
             dma((2, chunks)),
             dma((2, chunks)),
             pltpu.SemaphoreType.REGULAR((3,)),

time: 40.8 us -> 38.9 us (0.953)
  Pallas kernels: 39.3 us -> 37.5 us
    pallas_call x1, Pallas kernels: 39.3 us -> 37.5 us  [local(): pl.pallas_call(functools.partial(body, members, shards), out_shape=pltpu....]
where the time goes in v4:
time: 38.9 us; the launch traced here: 38.8 us
  Pallas kernels  37.5 us (96%)
  local copies, waits for them, and re-layouts  0.68 us (2%)
  between operations  0.66 us (2%)
    pallas_call x1, Pallas kernels, local(): pl.pallas_call(functools.partial(body, members, shards), out_shape=pltpu....  37.5 us

profile of v4, /device:TPU:1, one launch (start us, length us, event | category | flops | bytes accessed | tf_op | source)
XLA Modules:
  0.0 38.8 jit_solution(1740557041736788396)
XLA Ops:
  0.7 37.5 %shard_map.109 = f32[1,48,1024]{2,1,0:T(8,128)S(1)} custom-call(bf16[1,48,1024]{2,1,0:T(8,128)(2,1)} %lat_hbm.1, bf16[256,1024]{1,0:T(8,128)(2,1)} %emb_hbm.1, bf16[1024,1024]{1,0:T(8,128)(2,1)} %wmsg_hbm.1, bf16[1024,128]{1,0:T(8,128)(2,1)} %wout_hbm.1, s32[3,32]{1,0:T(4,128)} %need_hbm.1, s32[768]{0:T(1024)} %src_hbm.1, s32[768]{0:T(1024)} %dst_hbm.1, ...), custom_call_target="tpu_custom_call" | custom-call | flops 6000000000 | bytes 4000000 | tf_op jit(solution)/shard_map/pallas_call | solution.py:341
  38.1 0.7 %copy.13 = f32[1,48,1024]{2,1,0:T(8,128)} copy(f32[1,48,1024]{2,1,0:T(8,128)S(1)} %shard_map.109) | data formatting | bytes 393216

commit v5 on v4

--- a/solution.py
+++ b/solution.py
@@ -59,6 +59,8 @@
     truth,
     pw,
     fw,
+    need_nbr,
+    put,
     nbr,
     pre,
     od,
@@ -83,6 +85,8 @@
     load_sem,
     lat_send,
     lat_recv,
+    need_send,
+    need_recv,
     ens_send,
     ens_recv,
     gf_send,
@@ -140,7 +144,38 @@
         copy.start()
         loads.append(copy)
 
-    for copy in loads[:4]:
+    loads[4].wait()
+    pl.semaphore_wait(barrier, 5)
+    lat_copies = []
+    for side, neighbour in ((1, left), (0, right)):
+        copy = pltpu.make_async_remote_copy(
+            src_ref=lat,
+            dst_ref=nbr.at[pl.ds(side * node_dev, node_dev)],
+            send_sem=lat_send.at[side],
+            recv_sem=lat_recv.at[side],
+            device_id={"grid": neighbour},
+            device_id_type=MESH,
+        )
+        copy.start()
+        lat_copies.append(copy)
+
+    loads[2].wait()
+    need_copies = []
+    for side, neighbour in ((1, left), (0, right)):
+        copy = pltpu.make_async_remote_copy(
+            src_ref=need,
+            dst_ref=need_nbr.at[side],
+            send_sem=need_send.at[side],
+            recv_sem=need_recv.at[side],
+            device_id={"grid": neighbour},
+            device_id_type=MESH,
+        )
+        copy.start()
+        need_copies.append(copy)
+
+    for other in (ring(2), ring(-2)):
+        pl.semaphore_signal(relay.at[0], inc=1, device_id={"member": other}, device_id_type=MESH)
+    for copy in loads[:2] + loads[3:4]:
         copy.wait()
     lane = lax.broadcasted_iota(jnp.int32, (1, edges), 1)
     dest = jnp.where(lane < count[0], dst[...].reshape(1, edges), -1)
@@ -162,27 +197,12 @@
         axis=1,
     )
     place = onehot(lax.broadcasted_iota(jnp.int32, (3 * node_dev, 128), 0) == code)
-    nt[...] = dot(place, os_t).astype(BF16)
+    nt[:slots, :] = os_t[:slots]
+    nt[slots : 2 * slots, :] = os_t[2 * slots : 3 * slots]
+    nt[2 * slots :, :] = dot(place[2 * node_dev :], os_t).astype(BF16)
     n_lr[...] = dot(os_n, place[: 2 * node_dev], NT).astype(BF16)
     n_own = dot(os_n, place[2 * node_dev :], NT).astype(BF16)
 
-    loads[4].wait()
-    pl.semaphore_wait(barrier, 5)
-    lat_copies = []
-    for side, neighbour in ((1, left), (0, right)):
-        copy = pltpu.make_async_remote_copy(
-            src_ref=lat,
-            dst_ref=nbr.at[pl.ds(side * node_dev, node_dev)],
-            send_sem=lat_send.at[side],
-            recv_sem=lat_recv.at[side],
-            device_id={"grid": neighbour},
-            device_id_type=MESH,
-        )
-        copy.start()
-        lat_copies.append(copy)
-
-    for other in (ring(2), ring(-2)):
-        pl.semaphore_signal(relay.at[0], inc=1, device_id={"member": other}, device_id_type=MESH)
     loads[5].wait()
     for c in range(chunks):
         pre[:, cols(c)] = dot(od[...], emb[:, cols(c)]) + dot(n_own, lat[:, cols(c)])
@@ -271,6 +291,10 @@
         copy.start()
     gf[rows_me, :] = grads[0]
     arrived(ens, ens_send)
+    for copy in need_copies:
+        copy.wait()
+    theirs = jnp.concatenate([need_nbr[0, 2:3, :], need_nbr[1, 0:1, :]], axis=1)
+    put[...] = onehot(lax.broadcasted_iota(jnp.int32, (node_dev, 2 * slots), 0) == theirs)
     arrived(gsend, gf_recv)
 
     got = gf[...]
@@ -292,12 +316,12 @@
             grad = point_grads(c + 2)
         grad_pre = (spread * pre[:, cols(c)]).astype(BF16)
         rows = dot(nt[...], grad_pre)
-        rsend[:, cols(c)] = rows[: 2 * node_dev].astype(BF16)
-        own[:, cols(c)] = rows[2 * node_dev :]
+        rsend[:, cols(c)] = rows[: 2 * slots].astype(BF16)
+        own[:, cols(c)] = rows[2 * slots :]
         for side, neighbour in ((0, left), (1, right)):
             copy = pltpu.make_async_remote_copy(
-                src_ref=rsend.at[pl.ds(side * node_dev, node_dev), cols(c)],
-                dst_ref=back.at[side, :, cols(c)],
+                src_ref=rsend.at[pl.ds(side * slots, slots), cols(c)],
+                dst_ref=back.at[pl.ds((1 - side) * slots, slots), cols(c)],
                 send_sem=back_send.at[side, c],
                 recv_sem=back_recv.at[side, c],
                 device_id={"grid": neighbour},
@@ -306,12 +330,9 @@
             copy.start()
             back_copies.append(copy)
     arrived(gsend, gf_send)
-    for c in range(chunks):
-        for copy in back_copies[2 * c : 2 * c + 2]:
-            copy.wait_recv()
-        out[0, :, cols(c)] = (
-            own[:, cols(c)] + back[0, :, cols(c)].astype(F32) + back[1, :, cols(c)].astype(F32)
-        )
+    for copy in back_copies:
+        copy.wait_recv()
+    out[0] = own[...] + dot(put[...], back[...])
     for copy in back_copies:
         copy.wait_send()
 
@@ -335,6 +356,7 @@
     points = dst_embed.shape[0]
     edges = edge_src.shape[0]
     fields = w_out.shape[1]
+    slots = need_rows.shape[1]
     share = points // members
     chunks = width // 256
     dma = pltpu.SemaphoreType.DMA
@@ -355,12 +377,14 @@
             pltpu.VMEM((share, fields), F32),
             pltpu.VMEM((points,), F32),
             pltpu.VMEM((fields,), F32),
+            pltpu.VMEM((2,) + need_rows.shape, jnp.int32),
+            pltpu.VMEM((node_dev, 2 * slots), BF16),
             pltpu.VMEM((2 * node_dev, width), BF16),
             pltpu.VMEM((edges, width), F32),
             pltpu.VMEM((edges, points), BF16),
             pltpu.VMEM((points, edges), BF16),
             pltpu.VMEM((edges, 2 * node_dev), BF16),
-            pltpu.VMEM((3 * node_dev, edges), BF16),
+            pltpu.VMEM((2 * slots + node_dev, edges), BF16),
             pltpu.VMEM((points, width), BF16),
             pltpu.VMEM((points, width), F32),
             pltpu.VMEM((points, width), BF16),
@@ -372,11 +396,13 @@
             pltpu.VMEM((points, fields), BF16),
             pltpu.VMEM((2 * fields, width), BF16),
             pltpu.VMEM((points, width), F32),
-            pltpu.VMEM((2 * node_dev, width), BF16),
+            pltpu.VMEM((2 * slots, width), BF16),
             pltpu.VMEM((node_dev, width), F32),
-            pltpu.VMEM((2, node_dev, width), BF16),
+            pltpu.VMEM((2 * slots, width), BF16),
             pltpu.VMEM((points, 128), F32),
             dma((11,)),
+            dma((2,)),
+            dma((2,)),
             dma((2,)),
             dma((2,)),
             dma,

time: 38.9 us -> 38.7 us (level)
  no operation moved by 1% of the time
where the time goes in v5:
time: 38.7 us; the launch traced here: 38.6 us
  Pallas kernels  37.2 us (96%)
  local copies, waits for them, and re-layouts  0.68 us (2%)
  between operations  0.66 us (2%)
    pallas_call x1, Pallas kernels, local(): pl.pallas_call(functools.partial(body, members, shards), out_shape=pltpu....  37.2 us

profile of v5, /device:TPU:1, one launch (start us, length us, event | category | flops | bytes accessed | tf_op | source)
XLA Modules:
  0.0 38.6 jit_solution(13414909328712807607)
XLA Ops:
  0.7 37.2 %shard_map.109 = f32[1,48,1024]{2,1,0:T(8,128)S(1)} custom-call(bf16[1,48,1024]{2,1,0:T(8,128)(2,1)} %lat_hbm.1, bf16[256,1024]{1,0:T(8,128)(2,1)} %emb_hbm.1, bf16[1024,1024]{1,0:T(8,128)(2,1)} %wmsg_hbm.1, bf16[1024,128]{1,0:T(8,128)(2,1)} %wout_hbm.1, s32[3,32]{1,0:T(4,128)} %need_hbm.1, s32[768]{0:T(1024)} %src_hbm.1, s32[768]{0:T(1024)} %dst_hbm.1, ...), custom_call_target="tpu_custom_call" | custom-call | flops 6000000000 | bytes 4000000 | tf_op jit(solution)/shard_map/pallas_call | solution.py:363
  37.9 0.7 %copy.13 = f32[1,48,1024]{2,1,0:T(8,128)} copy(f32[1,48,1024]{2,1,0:T(8,128)S(1)} %shard_map.109) | data formatting | bytes 393216
